TPU v7x, 256 devices: a whole 4x4x8 slice. The times are simulated.
256 devices in a mesh: var: 32 (over z_lo, x, core), tp: 8 (over z_hi, y).
Axes of the slice: x: 4, y: 4, z: 8 (z_hi: 2, z_lo: 4; z = z_hi * 4 + z_lo), core: 2. Of those that a mesh axis runs over, the one named last changes fastest.
Arguments:
- parent_inputs: bfloat16 [4096, 256], P('var'), may hold values from -6 to 6
- gate_parent: bfloat16 [4096, 7168], P('var', 'tp'), may hold values from -0.09375 to 0.09375
- up_parent: bfloat16 [4096, 7168], P('var', 'tp'), may hold values from -0.09375 to 0.09375
- down_parent: bfloat16 [7168, 4096], P('tp', 'var'), may hold values from -0.0625 to 0.0625
- targets: bfloat16 [256, 4096], P('var', 'tp'), may hold values from -6 to 6
- widths: int32 [32], P('var'), may hold values from 1792 to 7168, as said below
- gains: float32 [32, 7168], P('var', 'tp'), may hold values from 0.25 to 2
Outputs:
- down_grad: bfloat16 [32, 7168, 4096], P('var', 'tp')
- gain_grad: float32 [32, 7168], P('var', 'tp')
Inputs may be any that keep to these rules, and one draw needn't show every extreme that they name: `widths`: every draw has a variant of exactly 7168 and one of exactly 1792 kept hidden units.
All inputs are finite; a program needn't handle non-finite values.
Results may differ from a plain program's by a relative error of at most 0.0059.
Values may be sent and summed in bfloat16 or wider, within the bound.
No kernel may reach another device: no remote copies, remote signals or barrier semaphores. Data moves between devices by JAX's collectives and lax.ppermute only.
A program may use at most 128 MiB of HBM per device.

v0:
```python
import jax
import jax.numpy as jnp
from jax import lax
from jax.sharding import PartitionSpec as P


def local(parent_inputs, gate_parent, up_parent, down_parent, targets, widths, gains):
    contract_rows = (((0,), (0,)), ((), ()))
    rows = parent_inputs.shape[1]
    local_ff = gate_parent.shape[1]
    feats = lax.all_gather(parent_inputs, "var", axis=0, tiled=True)
    gate_piece = lax.all_gather(gate_parent, "var", axis=0, tiled=True)
    up_piece = lax.all_gather(up_parent, "var", axis=0, tiled=True)
    gate_sum = lax.dot_general(feats, gate_piece, contract_rows, preferred_element_type=jnp.float32)
    up_sum = lax.dot_general(feats, up_piece, contract_rows, preferred_element_type=jnp.float32)
    raw = jax.nn.silu(gate_sum) * up_sum
    column = lax.axis_index("tp") * local_ff + lax.broadcasted_iota(jnp.int32, (1, local_ff), 1)
    kept = (column < widths[0]).astype(jnp.float32)
    hidden = (raw * gains * kept).astype(jnp.bfloat16)
    down_whole = lax.all_gather(down_parent, "var", axis=1, tiled=True)
    partial_value = jnp.dot(hidden, down_whole, preferred_element_type=jnp.float32)
    target_part = lax.all_gather(targets, "var", axis=0, tiled=True)
    output = lax.psum(partial_value, "tp")
    target_whole = lax.all_gather(target_part, "tp", axis=1, tiled=True)
    residual = (output - target_whole.astype(jnp.float32)).astype(jnp.bfloat16)
    scale = 1.0 / rows**0.5
    grad_down = lax.dot_general(hidden, residual, contract_rows, preferred_element_type=jnp.float32)
    grad_down = (grad_down * scale).astype(jnp.bfloat16)[None]
    back = lax.dot_general(
        residual, down_whole, (((1,), (1,)), ((), ())), preferred_element_type=jnp.float32
    )
    grad_gain = kept * jnp.sum(raw * back, axis=0, keepdims=True) * scale
    return (grad_down, grad_gain)


def solution(mesh):
    return jax.shard_map(
        local,
        mesh=mesh,
        in_specs=(
            P("var", None),
            P("var", "tp"),
            P("var", "tp"),
            P("tp", "var"),
            P("var", "tp"),
            P("var"),
            P("var", "tp"),
        ),
        out_specs=(P("var", "tp", None), P("var", "tp")),
        check_vma=False,
    )
```

profile of v0, /device:TPU:1, one launch (start us, length us, event | category | flops | bytes accessed | tf_op | source)
XLA Modules:
  0.0 589.8 jit_solution(13577693330374438191)
XLA Ops:
  7.2 0.0 all-gather.6.cloned.1.call-start
  7.2 0.7 all-gather.6.cloned.1.call-update
  7.9 0.0 all-gather.8.cloned.1.call-start
  7.9 0.7 all-gather.8.cloned.1.call-update
  8.6 0.0 all-gather.10.cloned.1.call-start
  8.7 0.7 all-gather.10.cloned.1.call-update
  9.4 0.0 all-gather.12.cloned.1.call-start
  9.4 0.5 all-gather.12.cloned.1.call-update
  10.0 0.0 all-gather.14.cloned.1.call-start
  10.0 49.5 %all_gather.22 = bf16[256,512]{1,0:T(8,128)(2,1)} all-gather(bf16[8,512]{1,0:T(8,128)(2,1)} %param.11), channel_id=1, replica_groups=mesh['var'=32,'tp'=8] {'var'}, dimensions={0}, use_global_device_ids=true | all-gather | bytes 270336 | tf_op jit(solution)/shard_map/all_gather | solution.py:22
  59.5 0.0 all-gather.14.cloned.1.call-update
  59.5 0.0 all-reduce.2.cloned.1.call-start
  60.2 0.7 reduce
  60.9 13.4 %all-gather.6.cloned.1.call-done = bf16[4096,256]{1,0:T(8,128)(2,1)} async-done(((bf16[128,256]{1,0:T(8,128)(2,1)}), bf16[4096,256]{1,0:T(8,128)(2,1)}) %all-gather.6.cloned.1.call-update) | async-done | bytes 2097168 | tf_op jit(solution)/shard_map/all_gather | solution.py:11
  74.4 0.0 copy-start
  74.4 69.0 %all-gather.8.cloned.1.call-done = bf16[4096,896]{1,0:T(8,128)(2,1)} async-done(((bf16[128,896]{1,0:T(8,128)(2,1)}), bf16[4096,896]{1,0:T(8,128)(2,1)}) %all-gather.8.cloned.1.call-update) | async-done | bytes 7340048 | tf_op jit(solution)/shard_map/all_gather | solution.py:12
  143.3 7.0 %fusion.5 = f32[256,896]{1,0:T(8,128)} fusion(bf16[4096,256]{1,0:T(8,128)(2,1)} %all-gather.6.cloned.1.call-done, bf16[4096,896]{1,0:T(8,128)(2,1)} %all-gather.8.cloned.1.call-done), kind=kOutput, calls=%fused_computation.12 | convolution fusion | flops 1879048192 | bytes 10354688 | tf_op jit(solution)/shard_map/dot_general | solution.py:14
  150.3 61.7 %all-gather.10.cloned.1.call-done = bf16[4096,896]{1,0:T(8,128)(2,1)} async-done(((bf16[128,896]{1,0:T(8,128)(2,1)}), bf16[4096,896]{1,0:T(8,128)(2,1)}) %all-gather.10.cloned.1.call-update) | async-done | bytes 7340048 | tf_op jit(solution)/shard_map/all_gather | solution.py:13
  212.1 0.0 copy-done
  212.1 5.7 convolution_multiply_fusion.1
  217.7 77.8 %all-gather.12.cloned.1.call-done = bf16[896,4096]{1,0:T(8,128)(2,1)} async-done(((bf16[896,128]{1,0:T(8,128)(2,1)}), bf16[896,4096]{1,0:T(8,128)(2,1)}) %all-gather.12.cloned.1.call-update) | async-done | bytes 7340048 | tf_op jit(solution)/shard_map/all_gather | solution.py:20
  295.5 7.4 %fusion.2 = f32[256,4096]{1,0:T(8,128)} fusion(bf16[896,4096]{1,0:T(8,128)(2,1)} %all-gather.12.cloned.1.call-done, f32[256,896]{1,0:T(8,128)S(1)} %convolution_multiply_fusion.1, f32[896]{0:T(1024)S(1)} %fusion.3, f32[896]{0:T(1024)S(1)} %reduce), kind=kOutput, calls=%fused_computation.7 | convolution fusion | flops 1879736320 | bytes 12459008 | tf_op jit(solution)/shard_map/dot_general | solution.py:21
  303.0 0.0 all-reduce.2.cloned.1.call-update
  303.0 68.9 %all-gather.14.cloned.1.call-done = bf16[256,4096]{1,0:T(8,128)(2,1)} async-done(((bf16[256,512]{1,0:T(8,128)(2,1)}), bf16[256,4096]{1,0:T(8,128)(2,1)}) %all-gather.14.cloned.1.call-update) | async-done | bytes 2097168 | tf_op jit(solution)/shard_map/all_gather | solution.py:24
  371.9 0.0 copy-start.2
  371.9 197.8 %all-reduce.2.cloned.1.call-done = f32[256,4096]{1,0:T(8,128)} async-done(((f32[256,4096]{1,0:T(8,128)}), f32[256,4096]{1,0:T(8,128)}) %all-reduce.2.cloned.1.call-update) | async-done | bytes 4194320 | tf_op jit(solution)/shard_map/psum | solution.py:23
  569.7 0.0 copy-start.1
  569.7 7.4 %fusion.1 = f32[896]{0:T(1024)S(1)} fusion(f32[256,896]{1,0:T(8,128)S(1)} %convolution_multiply_fusion.1, bf16[896,4096]{1,0:T(8,128)(2,1)} %all-gather.12.cloned.1.call-done, f32[256,4096]{1,0:T(8,128)} %all-reduce.2.cloned.1.call-done, bf16[256,4096]{1,0:T(8,128)(2,1)} %all-gather.14.cloned.1.call-done), kind=kOutput, calls=%fused_computation.5 | convolution fusion | flops 1882651776 | bytes 14552576 | tf_op jit(solution)/shard_map/dot_general | solution.py:29
  577.1 0.6 fusion.4
  577.7 0.0 copy-done.2
  577.7 0.0 copy-done.1
  577.7 5.2 fusion
  (1 shorter events, 0.0 us)
Async XLA Ops:
  7.2 67.2 %all-gather.6.cloned.1.call-start = ((), (), s32[]{:S(2)}) async-start(), calls=%async_computation | async-start | bytes 2162688 | tf_op jit(solution)/shard_map/all_gather | solution.py:11
  7.9 135.4 %all-gather.8.cloned.1.call-start = ((), (), s32[]{:S(2)}) async-start(), calls=%async_computation.1 | async-start | bytes 7569408 | tf_op jit(solution)/shard_map/all_gather | solution.py:12
  8.6 203.4 %all-gather.10.cloned.1.call-start = ((), (), s32[]{:S(2)}) async-start(), calls=%async_computation.2 | async-start | bytes 7569408 | tf_op jit(solution)/shard_map/all_gather | solution.py:13
  9.4 286.1 %all-gather.12.cloned.1.call-start = ((), (), s32[]{:S(2)}) async-start(), calls=%async_computation.3 | async-start | bytes 7569408 | tf_op jit(solution)/shard_map/all_gather | solution.py:20
  10.0 361.9 %all-gather.14.cloned.1.call-start = ((), (), s32[]{:S(2)}) async-start(), calls=%async_computation.5 | async-start | bytes 2359296 | tf_op jit(solution)/shard_map/all_gather | solution.py:24
  59.5 510.2 %all-reduce.2.cloned.1.call-start = ((), (), s32[]{:S(2)}) async-start(), calls=%async_computation.4 | async-start | bytes 8388608 | tf_op jit(solution)/shard_map/psum | solution.py:23
  74.4 137.7 %copy-start = (bf16[4096,256]{1,0:T(8,128)(2,1)S(1)}, bf16[4096,256]{1,0:T(8,128)(2,1)}, u32[]{:S(2)}) copy-start(bf16[4096,256]{1,0:T(8,128)(2,1)} %all-gather.6.cloned.1.call-done) | copy-start | bytes 6291460
  371.9 205.8 %copy-start.2 = (bf16[256,4096]{1,0:T(8,128)(2,1)S(1)}, bf16[256,4096]{1,0:T(8,128)(2,1)}, u32[]{:S(2)}) copy-start(bf16[256,4096]{1,0:T(8,128)(2,1)} %all-gather.14.cloned.1.call-done) | copy-start | bytes 6291460
  569.7 8.1 %copy-start.1 = (f32[256,4096]{1,0:T(8,128)S(1)}, f32[256,4096]{1,0:T(8,128)}, u32[]{:S(2)}) copy-start(f32[256,4096]{1,0:T(8,128)} %all-reduce.2.cloned.1.call-done) | copy-start | bytes 12582916
Sparse Core Ops, SparseCore 0:
  9.9 64.4 all-gather.5
  76.2 67.0 all-gather.7
  145.2 66.8 all-gather.9
  213.7 81.7 all-gather.11
  297.8 74.0 all-gather.13
  375.0 194.6 all-reduce.1
where the time goes:
time: 590 us
  waiting for transfers between devices  491 us (83%)
  blocking collectives  49.5 us (8%)
  matrix products  32.8 us (6%)
  between operations  14.8 us (3%)
    psum x1, waiting for transfers between devices, local(): output = lax.psum(partial_value, 'tp')  198 us
    all_gather x1, waiting for transfers between devices, local(): down_whole = lax.all_gather(down_parent, 'var', axis=1, tiled=True)  77.8 us
    all_gather x1, waiting for transfers between devices, local(): gate_piece = lax.all_gather(gate_parent, 'var', axis=0, tiled=True)  69 us
    all_gather x1, waiting for transfers between devices, local(): target_whole = lax.all_gather(target_part, 'tp', axis=1, tiled=True)  68.9 us
    all_gather x1, waiting for transfers between devices, local(): up_piece = lax.all_gather(up_parent, 'var', axis=0, tiled=True)  61.7 us
    all_gather x1, blocking collectives, local(): target_part = lax.all_gather(targets, 'var', axis=0, tiled=True)  49.5 us
    all_gather x1, waiting for transfers between devices, local(): feats = lax.all_gather(parent_inputs, 'var', axis=0, tiled=True)  13.4 us
  transfers between devices with their start and end apart: 6, of which 6 were waited for; matrix products, arithmetic and copies ran while one was open for 4% of the time, Pallas kernels for 0%

commit v1 on v0

--- a/solution.py
+++ b/solution.py
@@ -20,7 +20,7 @@
     down_whole = lax.all_gather(down_parent, "var", axis=1, tiled=True)
     partial_value = jnp.dot(hidden, down_whole, preferred_element_type=jnp.float32)
     target_part = lax.all_gather(targets, "var", axis=0, tiled=True)
-    output = lax.psum(partial_value, "tp")
+    output = jnp.sum(lax.all_gather(partial_value, "tp"), axis=0)
     target_whole = lax.all_gather(target_part, "tp", axis=1, tiled=True)
     residual = (output - target_whole.astype(jnp.float32)).astype(jnp.bfloat16)
     scale = 1.0 / rows**0.5

time: 590 us -> 970 us (1.64)
  waiting for transfers between devices: 491 us -> 857 us
  other arithmetic: 1.3 us -> 15.5 us
    all_gather x0 -> x1, waiting for transfers between devices: none -> 523 us  [local(): output = jnp.sum(lax.all_gather(partial_value, 'tp'), axis=0)]
    psum x1 -> x0, waiting for transfers between devices: 198 us -> none  [local(): output = lax.psum(partial_value, 'tp')]
    all_gather x1, waiting for transfers between devices: 13.4 us -> 62.9 us  [local(): feats = lax.all_gather(parent_inputs, 'var', axis=0, tiled=True)]
    reduce_sum x0 -> x1, other arithmetic: none -> 14.2 us  [local(): output = jnp.sum(lax.all_gather(partial_value, 'tp'), axis=0)]
  transfers between devices with their start and end apart: 6 -> 6, of which waited for: 6 -> 6; matrix products, arithmetic and copies ran while one was open for 4% -> 3% of each run, Pallas kernels for 0% -> 0%
where the time goes in v1:
time: 970 us
  waiting for transfers between devices  857 us (88%)
  blocking collectives  49 us (5%)
  matrix products  32.8 us (3%)
  other arithmetic  15.5 us (2%)
  between operations  14.8 us (2%)
    all_gather x1, waiting for transfers between devices, local(): output = jnp.sum(lax.all_gather(partial_value, 'tp'), axis=0)  523 us
    all_gather x1, waiting for transfers between devices, local(): down_whole = lax.all_gather(down_parent, 'var', axis=1, tiled=True)  77.8 us
    all_gather x1, waiting for transfers between devices, local(): gate_piece = lax.all_gather(gate_parent, 'var', axis=0, tiled=True)  68.9 us
    all_gather x1, waiting for transfers between devices, local(): feats = lax.all_gather(parent_inputs, 'var', axis=0, tiled=True)  62.9 us
    all_gather x1, waiting for transfers between devices, local(): up_piece = lax.all_gather(up_parent, 'var', axis=0, tiled=True)  61.7 us
    all_gather x1, waiting for transfers between devices, local(): target_whole = lax.all_gather(target_part, 'tp', axis=1, tiled=True)  59.7 us
    all_gather x1, blocking collectives, local(): target_part = lax.all_gather(targets, 'var', axis=0, tiled=True)  49 us
  transfers between devices with their start and end apart: 6, of which 6 were waited for; matrix products, arithmetic and copies ran while one was open for 3% of the time, Pallas kernels for 0%

profile of v1, /device:TPU:1, one launch (start us, length us, event | category | flops | bytes accessed | tf_op | source)
XLA Modules:
  0.0 970.0 jit_solution(7862191432472152313)
XLA Ops:
  7.2 0.0 all-gather.8.cloned.1.call-start
  7.2 0.7 all-gather.8.cloned.1.call-update
  7.9 0.0 all-gather.10.cloned.1.call-start
  7.9 0.7 all-gather.10.cloned.1.call-update
  8.6 0.0 all-gather.12.cloned.1.call-start
  8.7 0.7 all-gather.12.cloned.1.call-update
  9.4 0.0 all-gather.14.cloned.1.call-start
  9.4 0.5 all-gather.14.cloned.1.call-update
  10.0 0.0 all-gather.18.cloned.1.call-start
  10.7 0.7 reduce
  11.4 62.9 %all-gather.8.cloned.1.call-done = bf16[4096,256]{1,0:T(8,128)(2,1)} async-done(((bf16[128,256]{1,0:T(8,128)(2,1)}), bf16[4096,256]{1,0:T(8,128)(2,1)}) %all-gather.8.cloned.1.call-update) | async-done | bytes 2097168 | tf_op jit(solution)/shard_map/all_gather | solution.py:11
  74.3 0.0 copy-start.1
  74.3 68.9 %all-gather.10.cloned.1.call-done = bf16[4096,896]{1,0:T(8,128)(2,1)} async-done(((bf16[128,896]{1,0:T(8,128)(2,1)}), bf16[4096,896]{1,0:T(8,128)(2,1)}) %all-gather.10.cloned.1.call-update) | async-done | bytes 7340048 | tf_op jit(solution)/shard_map/all_gather | solution.py:12
  143.2 7.0 fusion.5
  150.2 61.7 %all-gather.12.cloned.1.call-done = bf16[4096,896]{1,0:T(8,128)(2,1)} async-done(((bf16[128,896]{1,0:T(8,128)(2,1)}), bf16[4096,896]{1,0:T(8,128)(2,1)}) %all-gather.12.cloned.1.call-update) | async-done | bytes 7340048 | tf_op jit(solution)/shard_map/all_gather | solution.py:13
  211.9 0.0 copy-done.1
  211.9 5.7 convolution_multiply_fusion.1
  217.6 77.8 %all-gather.14.cloned.1.call-done = bf16[896,4096]{1,0:T(8,128)(2,1)} async-done(((bf16[896,128]{1,0:T(8,128)(2,1)}), bf16[896,4096]{1,0:T(8,128)(2,1)}) %all-gather.14.cloned.1.call-update) | async-done | bytes 7340048 | tf_op jit(solution)/shard_map/all_gather | solution.py:20
  295.4 7.4 fusion.2
  302.8 0.0 copy-start.3
  302.8 0.0 all-gather.18.cloned.1.call-update
  302.8 0.0 all-gather.16.cloned.1.call-start
  302.9 0.6 copy-done.3
  303.5 49.0 %all_gather.30 = bf16[256,512]{1,0:T(8,128)(2,1)} all-gather(bf16[8,512]{1,0:T(8,128)(2,1)S(1)} %copy-done.3), channel_id=1, replica_groups=mesh['var'=32,'tp'=8] {'var'}, dimensions={0}, use_global_device_ids=true | all-gather | bytes 270336 | tf_op jit(solution)/shard_map/all_gather | solution.py:22
  352.5 0.0 all-gather.16.cloned.1.call-update
  352.5 523.4 %all-gather.18.cloned.1.call-done = f32[2048,4096]{1,0:T(8,128)} async-done(((f32[256,4096]{1,0:T(8,128)}), f32[2048,4096]{1,0:T(8,128)}) %all-gather.18.cloned.1.call-update) | async-done | bytes 33554448 | tf_op jit(solution)/shard_map/all_gather | solution.py:23
  876.0 14.2 %reduce_sum.20 = f32[256,4096]{1,0:T(8,128)} reduce(f32[8,256,4096]{2,1,0:T(8,128)} %bitcast.12, f32[]{:T(128)} %constant.4.clone.1), dimensions={0}, to_apply=%region_0.1 | reduce | flops 7340032 | bytes 37748740 | tf_op jit(solution)/shard_map/reduce_sum | solution.py:23
  890.1 59.7 %all-gather.16.cloned.1.call-done = bf16[256,4096]{1,0:T(8,128)(2,1)} async-done(((bf16[256,512]{1,0:T(8,128)(2,1)}), bf16[256,4096]{1,0:T(8,128)(2,1)}) %all-gather.16.cloned.1.call-update) | async-done | bytes 2097168 | tf_op jit(solution)/shard_map/all_gather | solution.py:24
  949.9 0.0 copy-start
  949.9 0.0 copy-start.2
  949.9 7.4 fusion.1
  957.3 0.6 fusion.4
  957.9 0.0 copy-done
  957.9 0.0 copy-done.2
  957.9 5.2 fusion
  (1 shorter events, 0.0 us)
Async XLA Ops:
  7.2 67.1 %all-gather.8.cloned.1.call-start = ((), (), s32[]{:S(2)}) async-start(), calls=%async_computation | async-start | bytes 2162688 | tf_op jit(solution)/shard_map/all_gather | solution.py:11
  7.9 135.3 %all-gather.10.cloned.1.call-start = ((), (), s32[]{:S(2)}) async-start(), calls=%async_computation.1 | async-start | bytes 7569408 | tf_op jit(solution)/shard_map/all_gather | solution.py:12
  8.6 203.3 %all-gather.12.cloned.1.call-start = ((), (), s32[]{:S(2)}) async-start(), calls=%async_computation.2 | async-start | bytes 7569408 | tf_op jit(solution)/shard_map/all_gather | solution.py:13
  9.4 286.0 %all-gather.14.cloned.1.call-start = ((), (), s32[]{:S(2)}) async-start(), calls=%async_computation.3 | async-start | bytes 7569408 | tf_op jit(solution)/shard_map/all_gather | solution.py:20
  10.0 866.0 %all-gather.18.cloned.1.call-start = ((), (), s32[]{:S(2)}) async-start(), calls=%async_computation.5 | async-start | bytes 37748736 | tf_op jit(solution)/shard_map/all_gather | solution.py:23
  74.3 137.6 %copy-start.1 = (bf16[4096,256]{1,0:T(8,128)(2,1)S(1)}, bf16[4096,256]{1,0:T(8,128)(2,1)}, u32[]{:S(2)}) copy-start(bf16[4096,256]{1,0:T(8,128)(2,1)} %all-gather.8.cloned.1.call-done) | copy-start | bytes 6291460
  302.8 0.7 copy-start.3
  302.8 647.0 %all-gather.16.cloned.1.call-start = ((), (), s32[]{:S(2)}) async-start(), calls=%async_computation.4 | async-start | bytes 2359296 | tf_op jit(solution)/shard_map/all_gather | solution.py:24
  949.9 8.1 copy-start
  949.9 8.1 copy-start.2
Sparse Core Ops, SparseCore 0:
  9.9 64.3 all-gather.7
  76.1 67.0 all-gather.9
  145.0 66.8 all-gather.11
  213.5 81.7 all-gather.13
  302.9 572.9 all-gather.17
  878.3 71.5 all-gather.15
